TPU v7x, 128 devices: a whole 4x4x4 slice. The times are simulated.
128 devices in a mesh: row: 4 (over x), col: 8 (over y, core), layer: 4 (over z).
Axes of the slice: x: 4, y: 4, z: 4, core: 2. Of those that a mesh axis runs over, the one named last changes fastest.
Arguments:
- blocks: bfloat16 [512, 16, 128, 128], P(('row', 'col')), may hold values from -0.125 to 0.125
- flags: int32 [512, 16], P(('row', 'col')), may hold values 0 or 1
Outputs:
- next_blocks: bfloat16 [512, 16, 128, 128], P(('row', 'col', 'layer'))
All inputs are finite; a program needn't handle non-finite values. No bound on the sum of `flags` on one device may be relied on, other than what follows from the above.
Results may differ from a plain program's by a relative error of at most 0.0075.
Values may be sent and summed in bfloat16 or wider, within the bound.
A program may use at most 192 MiB of HBM per device.

v0:
```python
import jax
import jax.numpy as jnp
from jax import lax
from jax.sharding import PartitionSpec as P


def padded_2(block, sides, width):
    for axis, dim in sides:
        count = lax.axis_size(axis)
        forward = [(i, i + 1) for i in range(count - 1)]
        forward.append((count - 1, 0))
        backward = [(target, source) for source, target in forward]
        low = lax.ppermute(
            lax.slice_in_dim(block, block.shape[dim] - width, None, axis=dim), axis, forward
        )
        high = lax.ppermute(lax.slice_in_dim(block, 0, width, axis=dim), axis, backward)
        block = jnp.concatenate([low, block, high], axis=dim)
    return block


def banded_part(left, padded, first_offset, offsets, row_count):
    width = left.shape[1]
    half = width // 2
    block = left.shape[2]

    def step(index, total):
        offset = first_offset + index
        piece = lax.dynamic_slice(left, (0, offset + half, 0, 0), (row_count, 1, block, block))[
            :, 0
        ]
        moved = lax.dynamic_slice(
            padded, (offset + half, width - offset, 0, 0), (row_count, width, block, block)
        )
        return total + jnp.einsum(
            "nxy,nsyz->nsxz", piece, moved, preferred_element_type=jnp.float32
        )

    start = jnp.zeros((row_count, width, block, block), jnp.float32)
    return lax.fori_loop(0, offsets, step, start)


def pad_slots(rimmed):
    width = rimmed.shape[1]
    return jnp.pad(rimmed, ((0, 0), (width, width), (0, 0), (0, 0)))


def per_device(blocks, flags):
    nrows = blocks.shape[0]
    width = blocks.shape[1]
    block = blocks.shape[2]
    half = width // 2
    layers = lax.axis_size("layer")
    layer_at = lax.axis_index("layer")
    quarter = nrows // layers
    share = width // layers
    slots = jnp.arange(width, dtype=jnp.int32)
    centre = (slots == half).astype(jnp.int32)
    keep_int = jnp.maximum(flags, centre[None, :])
    keep_wide = keep_int.astype(jnp.float32)[:, :, None, None]
    filtered = blocks * keep_int.astype(jnp.bfloat16)[:, :, None, None]
    ident = jnp.where(
        (slots == half)[:, None, None], jnp.eye(block, dtype=jnp.float32)[None], jnp.float32(0.0)
    )
    rimmed = padded_2(filtered, ((("row", "col"), 0),), half)
    padded_x = pad_slots(rimmed)
    first_offset = layer_at * share - half
    term = banded_part(filtered, padded_x, first_offset, share, lax.axis_size("layer") * quarter)
    square = lax.psum_scatter(
        (term * keep_wide).astype(jnp.bfloat16), "layer", scatter_dimension=0, tiled=True
    ).astype(jnp.float32)
    third_own = (3.0 * ident[None] - square).astype(jnp.bfloat16)
    third = lax.all_gather(third_own, "layer", axis=0, tiled=True)
    third_rim = padded_2(third, ((("row", "col"), 0),), half)
    padded_t = pad_slots(third_rim)
    term = banded_part(filtered, padded_t, first_offset, share, quarter * lax.axis_size("layer"))
    result = lax.psum_scatter(term * keep_wide, "layer", scatter_dimension=0, tiled=True)
    return (0.5 * result).astype(jnp.bfloat16)


def solution(mesh):
    return jax.shard_map(
        per_device,
        mesh=mesh,
        in_specs=(P(("row", "col"), None, None, None), P(("row", "col"), None)),
        out_specs=P(("row", "col", "layer"), None, None, None),
        check_vma=False,
    )
```

profile of v0, /device:TPU:0, one launch (start us, length us, event | category | flops | bytes accessed | tf_op | source)
XLA Modules:
  0.0 705.0 jit_solution(13777873598402649877)
XLA Ops:
  6.5 0.7 maximum_convert_fusion
  7.2 0.1 copy.9
  7.3 7.2 %copy_multiply_fusion = bf16[16,16,128,128]{3,2,0,1:T(8,128)(2,1)} fusion(bf16[16,16,128,128]{3,2,1,0:T(8,128)(2,1)} %param.6, bf16[16,16]{0,1:T(8,128)(2,1)S(1)} %copy.9), kind=kLoop, calls=%fused_computation.28 | loop fusion | flops 4194304 | bytes 16777728 | tf_op jit(solution)/shard_map/mul | solution.py:60
  14.5 6.0 fusion.23
  20.6 5.1 collective-permute-start.1
  25.6 46.5 %collective-permute-done = bf16[8,16,128,128]{3,2,0,1:T(8,128)(2,1)} collective-permute-done((bf16[8,16,128,128]{3,2,0,1:T(8,128)(2,1)}, bf16[8,16,128,128]{3,2,0,1:T(8,128)(2,1)}, u32[]{:S(2)}, u32[]{:S(2)}) %collective-permute-start) | collective-permute-done | bytes 4194336 | tf_op jit(solution)/shard_map/ppermute | solution.py:13
  72.1 39.3 %fusion.17 = bf16[32,48,128,128]{3,2,0,1:T(8,128)(2,1)} fusion(bf16[8,16,128,128]{3,2,0,1:T(8,128)(2,1)} %collective-permute-done.1, bf16[16,16,128,128]{3,2,0,1:T(8,128)(2,1)} %copy_multiply_fusion, bf16[8,16,128,128]{3,2,0,1:T(8,128)(2,1)} %collective-permute-done), kind=kLoop, calls=%fused_computation.24 | loop fusion | flops 301989888 | bytes 67108864 | tf_op jit(solution)/shard_map/concatenate | solution.py:17
  111.4 57.6 %while.32 = (s32[]{:T(128)}, f32[16,16,128,128]{2,3,1,0:T(8,128)}, s32[]{:T(128)}, bf16[32,48,128,128]{3,2,0,1:T(8,128)(2,1)}, bf16[16,16,128,128]{3,2,0,1:T(8,1...) while((s32[]{:T(128)}, f32[16,16,128,128]{2,3,1,0:T(8,128)}, ...), condition=%wide.region_1.2_spmd.clone, body=%wide.region_0.1_spmd.clone.sunk | while | flops 1082130432 | bytes 42467592 | solution.py:39
  111.4 9.7 %bitcast_add_fusion.4 = f32[16,16,128,128]{2,3,1,0:T(8,128)} fusion(f32[16,16,128,128]{2,3,1,0:T(8,128)} %get-tuple-element.432, pred[]{:T(512)S(6)} %compare.88, bf16[16,16,128,128]{3,2,0,1:T(8,128)(2,1)} %get-tuple-element.447, s32[]{:T(128)S(6)} %select_n.82, bf16[32,48,128,128]{3,2,0,1:T(8,128)(2,1)} %get-tuple-element.446, s32[]{:T(128)S(6)} %select_n.83, ...), kind=kOutput, calls=%fused_computation.clone.1 | convolution fusion | flops 1082130432 | bytes 42467340 | tf_op jit(solution)/shard_map/while/body/eval_jaxpr/nxy,nsyz->nsxz/dot_general | solution.py:34
  121.2 15.9 %bitcast_add_fusion.4 = f32[16,16,128,128]{2,3,1,0:T(8,128)} fusion(f32[16,16,128,128]{2,3,1,0:T(8,128)} %get-tuple-element.432, pred[]{:T(512)S(6)} %compare.88, bf16[16,16,128,128]{3,2,0,1:T(8,128)(2,1)} %get-tuple-element.447, s32[]{:T(128)S(6)} %select_n.82, bf16[32,48,128,128]{3,2,0,1:T(8,128)(2,1)} %get-tuple-element.446, s32[]{:T(128)S(6)} %select_n.83, ...), kind=kOutput, calls=%fused_computation.clone.1 | convolution fusion | flops 1082130432 | bytes 42467340 | tf_op jit(solution)/shard_map/while/body/eval_jaxpr/nxy,nsyz->nsxz/dot_general | solution.py:34
  137.1 15.9 %bitcast_add_fusion.4 = f32[16,16,128,128]{2,3,1,0:T(8,128)} fusion(f32[16,16,128,128]{2,3,1,0:T(8,128)} %get-tuple-element.432, pred[]{:T(512)S(6)} %compare.88, bf16[16,16,128,128]{3,2,0,1:T(8,128)(2,1)} %get-tuple-element.447, s32[]{:T(128)S(6)} %select_n.82, bf16[32,48,128,128]{3,2,0,1:T(8,128)(2,1)} %get-tuple-element.446, s32[]{:T(128)S(6)} %select_n.83, ...), kind=kOutput, calls=%fused_computation.clone.1 | convolution fusion | flops 1082130432 | bytes 42467340 | tf_op jit(solution)/shard_map/while/body/eval_jaxpr/nxy,nsyz->nsxz/dot_general | solution.py:34
  153.1 15.9 %bitcast_add_fusion.4 = f32[16,16,128,128]{2,3,1,0:T(8,128)} fusion(f32[16,16,128,128]{2,3,1,0:T(8,128)} %get-tuple-element.432, pred[]{:T(512)S(6)} %compare.88, bf16[16,16,128,128]{3,2,0,1:T(8,128)(2,1)} %get-tuple-element.447, s32[]{:T(128)S(6)} %select_n.82, bf16[32,48,128,128]{3,2,0,1:T(8,128)(2,1)} %get-tuple-element.446, s32[]{:T(128)S(6)} %select_n.83, ...), kind=kOutput, calls=%fused_computation.clone.1 | convolution fusion | flops 1082130432 | bytes 42467340 | tf_op jit(solution)/shard_map/while/body/eval_jaxpr/nxy,nsyz->nsxz/dot_general | solution.py:34
  169.0 17.6 %copy.12 = f32[16,16,128,128]{3,2,1,0:T(8,128)} copy(f32[16,16,128,128]{2,3,1,0:T(8,128)} %get-tuple-element.273) | data formatting | bytes 33554432 | tf_op jit(solution)/shard_map/while | solution.py:39
  186.7 9.2 %multiply_convert_fusion = bf16[16,16,128,128]{3,2,1,0:T(8,128)(2,1)} fusion(f32[16,16,128,128]{3,2,1,0:T(8,128)} %copy.12, f32[16,16]{1,0:T(8,128)S(1)} %get-tuple-element.355), kind=kLoop, calls=%fused_computation.27 | loop fusion | flops 8388608 | bytes 25166848 | tf_op jit(solution)/shard_map/convert_element_type | solution.py:69
  195.9 0.0 all-gather.2.cloned.1.call-start
  196.0 0.1 select_multiply_fusion
  196.2 82.4 %reduce-scatter.3.cloned.1.call-done = bf16[4,16,128,128]{3,2,1,0:T(8,128)(2,1)} async-done(((bf16[16,16,128,128]{3,2,1,0:T(8,128)(2,1)}), bf16[4,16,128,128]{3,2,1,0:T(8,128)(2,1)}) %reduce-scatter.3.cloned.1.call-update) | async-done | bytes 2097168 | tf_op jit(solution)/shard_map/reduce_scatter | solution.py:68
  278.6 3.7 subtract_convert_fusion
  282.3 83.0 %all-gather.2.cloned.1.call-done = bf16[16,16,128,128]{3,2,1,0:T(8,128)(2,1)} async-done(((bf16[4,16,128,128]{3,2,1,0:T(8,128)(2,1)}), bf16[16,16,128,128]{3,2,1,0:T(8,128)(2,1)}) %all-gather.2.cloned.1.call-update) | async-done | bytes 8388624 | tf_op jit(solution)/shard_map/all_gather | solution.py:72
  365.4 6.0 fusion.22
  371.4 5.1 collective-permute-start.3
  376.5 46.5 %collective-permute-done.2 = bf16[8,16,128,128]{3,2,1,0:T(8,128)(2,1)} collective-permute-done((bf16[8,16,128,128]{3,2,1,0:T(8,128)(2,1)}, bf16[8,16,128,128]{3,2,1,0:T(8,128)(2,1)}, u32[]{:S(2)}, u32[]{:S(2)}) %collective-permute-start.2) | collective-permute-done | bytes 4194336 | tf_op jit(solution)/shard_map/ppermute | solution.py:13
  423.0 35.9 %fusion.19 = bf16[32,48,128,128]{3,2,1,0:T(8,128)(2,1)} fusion(bf16[8,16,128,128]{3,2,1,0:T(8,128)(2,1)} %collective-permute-done.3, bf16[16,16,128,128]{3,2,1,0:T(8,128)(2,1)} %all-gather.2.cloned.1.call-done, bf16[8,16,128,128]{3,2,1,0:T(8,128)(2,1)} %collective-permute-done.2), kind=kLoop, calls=%fused_computation.26 | loop fusion | flops 301989888 | bytes 67108864 | tf_op jit(solution)/shard_map/concatenate | solution.py:17
  458.9 57.6 %while.33 = (s32[]{:T(128)}, f32[16,16,128,128]{2,3,1,0:T(8,128)}, s32[]{:T(128)}, bf16[32,48,128,128]{3,2,1,0:T(8,128)(2,1)}, bf16[16,16,128,128]{3,2,0,1:T(8,1...) while((s32[]{:T(128)}, f32[16,16,128,128]{2,3,1,0:T(8,128)}, ...), condition=%wide.region_4.5_spmd.clone, body=%wide.region_3.4_spmd.clone.sunk | while | flops 1082130432 | bytes 42467592 | solution.py:39
  459.0 9.7 %bitcast_add_fusion.5 = f32[16,16,128,128]{2,3,1,0:T(8,128)} fusion(f32[16,16,128,128]{2,3,1,0:T(8,128)} %get-tuple-element.468, bf16[32,48,128,128]{3,2,1,0:T(8,128)(2,1)} %get-tuple-element.482, s32[]{:T(128)S(6)} %select_n.85, s32[]{:T(128)S(6)} %select_n.86, pred[]{:T(512)S(6)} %compare.89, bf16[16,16,128,128]{3,2,0,1:T(8,128)(2,1)} %get-tuple-element.483, ...), kind=kOutput, calls=%fused_computation.6.clone.1 | convolution fusion | flops 1082130432 | bytes 42467340 | tf_op jit(solution)/shard_map/while/body/eval_jaxpr/nxy,nsyz->nsxz/dot_general | solution.py:34
  468.7 16.0 %bitcast_add_fusion.5 = f32[16,16,128,128]{2,3,1,0:T(8,128)} fusion(f32[16,16,128,128]{2,3,1,0:T(8,128)} %get-tuple-element.468, bf16[32,48,128,128]{3,2,1,0:T(8,128)(2,1)} %get-tuple-element.482, s32[]{:T(128)S(6)} %select_n.85, s32[]{:T(128)S(6)} %select_n.86, pred[]{:T(512)S(6)} %compare.89, bf16[16,16,128,128]{3,2,0,1:T(8,128)(2,1)} %get-tuple-element.483, ...), kind=kOutput, calls=%fused_computation.6.clone.1 | convolution fusion | flops 1082130432 | bytes 42467340 | tf_op jit(solution)/shard_map/while/body/eval_jaxpr/nxy,nsyz->nsxz/dot_general | solution.py:34
  484.6 16.0 %bitcast_add_fusion.5 = f32[16,16,128,128]{2,3,1,0:T(8,128)} fusion(f32[16,16,128,128]{2,3,1,0:T(8,128)} %get-tuple-element.468, bf16[32,48,128,128]{3,2,1,0:T(8,128)(2,1)} %get-tuple-element.482, s32[]{:T(128)S(6)} %select_n.85, s32[]{:T(128)S(6)} %select_n.86, pred[]{:T(512)S(6)} %compare.89, bf16[16,16,128,128]{3,2,0,1:T(8,128)(2,1)} %get-tuple-element.483, ...), kind=kOutput, calls=%fused_computation.6.clone.1 | convolution fusion | flops 1082130432 | bytes 42467340 | tf_op jit(solution)/shard_map/while/body/eval_jaxpr/nxy,nsyz->nsxz/dot_general | solution.py:34
  500.6 16.0 %bitcast_add_fusion.5 = f32[16,16,128,128]{2,3,1,0:T(8,128)} fusion(f32[16,16,128,128]{2,3,1,0:T(8,128)} %get-tuple-element.468, bf16[32,48,128,128]{3,2,1,0:T(8,128)(2,1)} %get-tuple-element.482, s32[]{:T(128)S(6)} %select_n.85, s32[]{:T(128)S(6)} %select_n.86, pred[]{:T(512)S(6)} %compare.89, bf16[16,16,128,128]{3,2,0,1:T(8,128)(2,1)} %get-tuple-element.483, ...), kind=kOutput, calls=%fused_computation.6.clone.1 | convolution fusion | flops 1082130432 | bytes 42467340 | tf_op jit(solution)/shard_map/while/body/eval_jaxpr/nxy,nsyz->nsxz/dot_general | solution.py:34
  516.5 17.6 %copy.14 = f32[16,16,128,128]{3,2,1,0:T(8,128)} copy(f32[16,16,128,128]{2,3,1,0:T(8,128)} %get-tuple-element.274) | data formatting | bytes 33554432 | tf_op jit(solution)/shard_map/while | solution.py:39
  534.2 11.4 %broadcast_multiply_fusion = f32[16,16,128,128]{3,2,1,0:T(8,128)} fusion(f32[16,16,128,128]{3,2,1,0:T(8,128)} %copy.14, f32[16,16]{1,0:T(8,128)S(1)} %get-tuple-element.355), kind=kLoop, calls=%fused_computation.29 | loop fusion | flops 4194304 | bytes 33555456 | tf_op jit(solution)/shard_map/mul | solution.py:76
  545.6 148.8 %reduce-scatter.5.cloned.1.call-done = f32[4,16,128,128]{3,2,1,0:T(8,128)} async-done(((f32[16,16,128,128]{3,2,1,0:T(8,128)}), f32[4,16,128,128]{3,2,1,0:T(8,128)}) %reduce-scatter.5.cloned.1.call-update) | async-done | bytes 4194320 | tf_op jit(solution)/shard_map/reduce_scatter | solution.py:76
  694.4 4.0 multiply_convert_fusion.1
  (14 shorter events, 0.1 us)
Async XLA Ops:
  6.5 272.1 %reduce-scatter.3.cloned.1.call-start = ((), (), s32[]{:S(2)}) async-start(), calls=%async_computation.2 | async-start | bytes 10485760 | tf_op jit(solution)/shard_map/reduce_scatter | solution.py:68
  20.6 51.6 %collective-permute-start = (bf16[8,16,128,128]{3,2,0,1:T(8,128)(2,1)}, bf16[8,16,128,128]{3,2,0,1:T(8,128)(2,1)}, u32[]{:S(2)}, u32[]{:S(2)}) collective-permute-start(bf16[8,16,128,128]{3,2,0,1:T(8,128)(2,1)} %get-tuple-element.353), channel_id=1, source_target_pairs={{0,4},{4,8},{8,12},{12,16},{16,20},{20,24},{24,28},{28,32},{32,36}... | collective-permute-start | bytes 12582920 | tf_op jit(solution)/shard_map/ppermute | solution.py:13
  20.6 51.6 %collective-permute-start.1 = (bf16[8,16,128,128]{3,2,0,1:T(8,128)(2,1)}, bf16[8,16,128,128]{3,2,0,1:T(8,128)(2,1)}, u32[]{:S(2)}, u32[]{:S(2)}) collective-permute-start(bf16[8,16,128,128]{3,2,0,1:T(8,128)(2,1)} %get-tuple-element.354), channel_id=1, source_target_pairs={{4,0},{8,4},{12,8},{16,12},{20,16},{24,20},{28,24},{32,28},{36,32}... | collective-permute-start | bytes 12582920 | tf_op jit(solution)/shard_map/ppermute | solution.py:16
  195.9 169.4 %all-gather.2.cloned.1.call-start = ((), (), s32[]{:S(2)}) async-start(), calls=%async_computation.3 | async-start | bytes 10485760 | tf_op jit(solution)/shard_map/all_gather | solution.py:72
  282.3 412.1 %reduce-scatter.5.cloned.1.call-start = ((), (), s32[]{:S(2)}) async-start(), calls=%async_computation.4 | async-start | bytes 20971520 | tf_op jit(solution)/shard_map/reduce_scatter | solution.py:76
  371.4 51.6 %collective-permute-start.2 = (bf16[8,16,128,128]{3,2,1,0:T(8,128)(2,1)}, bf16[8,16,128,128]{3,2,1,0:T(8,128)(2,1)}, u32[]{:S(2)}, u32[]{:S(2)}) collective-permute-start(bf16[8,16,128,128]{3,2,1,0:T(8,128)(2,1)} %get-tuple-element.351), channel_id=1, source_target_pairs={{0,4},{4,8},{8,12},{12,16},{16,20},{20,24},{24,28},{28,32},{32,36}... | collective-permute-start | bytes 12582920 | tf_op jit(solution)/shard_map/ppermute | solution.py:13
  371.4 51.6 %collective-permute-start.3 = (bf16[8,16,128,128]{3,2,1,0:T(8,128)(2,1)}, bf16[8,16,128,128]{3,2,1,0:T(8,128)(2,1)}, u32[]{:S(2)}, u32[]{:S(2)}) collective-permute-start(bf16[8,16,128,128]{3,2,1,0:T(8,128)(2,1)} %get-tuple-element.352), channel_id=1, source_target_pairs={{4,0},{8,4},{12,8},{16,12},{20,16},{24,20},{28,24},{32,28},{36,32}... | collective-permute-start | bytes 12582920 | tf_op jit(solution)/shard_map/ppermute | solution.py:16
Sparse Core Ops, SparseCore 0:
  196.0 82.4 reduce-scatter.2
  282.4 82.9 all-gather.1
  545.7 148.6 reduce-scatter.4
where the time goes:
time: 706 us; the launch traced here: 705 us
  waiting for transfers between devices  407 us (58%)
  matrix products  115 us (16%)
  other arithmetic  112 us (16%)
  local copies, waits for them, and re-layouts  47.4 us (7%)
  between operations  13.1 us (2%)
  starting transfers between devices  10.2 us (1%)
    reduce_scatter x1, waiting for transfers between devices, per_device(): lax.psum_scatter(term * keep_wide, 'layer', scatter_dimension=0, tiled=True)  149 us
    dot_general x8, matrix products, step(): jnp.einsum('nxy,nsyz->nsxz', piece, moved, preferred_element_type=jnp.flo...  115 us
    ppermute x2, waiting for transfers between devices, padded_2(): lax.ppermute(lax.slice_in_dim(block, block.shape[dim] - width, None, axis...  93 us
    all_gather x1, waiting for transfers between devices, per_device(): third = lax.all_gather(third_own, 'layer', axis=0, tiled=True)  83 us
    reduce_scatter x1, waiting for transfers between devices, per_device(): lax.psum_scatter((term * keep_wide).astype(jnp.bfloat16), 'layer', scatte...  82.4 us
    concatenate x2, other arithmetic, padded_2(): block = jnp.concatenate([low, block, high], axis=dim)  75.2 us
    while x2, local copies, waits for them, and re-layouts, banded_part(): return lax.fori_loop(0, offsets, step, start)  35.3 us
  transfers between devices with their start and end apart: 7, of which 5 were waited for; matrix products, arithmetic and copies ran while one was open for 0% of the time, Pallas kernels for 0%

commit v1 on v0

v1 whole, which is shorter than its diff:
```python
import functools

import jax
import jax.numpy as jnp
from jax import lax
from jax.experimental import pallas as pl
from jax.experimental.pallas import tpu as pltpu
from jax.sharding import PartitionSpec as P

MESH = pl.DeviceIdType.MESH
REACH = 4
DIAGS = range(-REACH, REACH + 1)
BS = 128
SB = 256
W = 16


def place(layer, kind, d):
    m = (d - layer + 3) >> 2
    t = (m + kind) & 1
    return layer - d + 4 * m + 4 * t, 1 + m + t


def spans(d):
    out = []
    for r in range(2):
        low, high = 2 * d - r + 8, 2 * d - r + 10
        first, last = max(low, 0), min(high, W)
        if last > first:
            out.append((r, first - low, first, last - first))
    return out


def kernel(x, flags, out, xc, xs, xl, xr, tr, os, load_c, load_x, send_x, recv_x, send_t, recv_t, send_o, recv_o, own_o):
    row, col, layer = lax.axis_index("row"), lax.axis_index("col"), lax.axis_index("layer")
    cols, layers = lax.axis_size("col"), lax.axis_size("layer")
    groups = lax.axis_size("row") * cols
    group = row * cols + col

    def at_group(step):
        there = lax.rem(group + step + groups, groups)
        return there // cols, lax.rem(there, cols), layer

    above, below = at_group(1), at_group(-1)

    def keep(i, s):
        return jnp.float32(1.0) if s == W // 2 else flags[i, s].astype(jnp.float32)

    def class_loads(kind):
        for d in DIAGS:
            i, _ = place(layer, kind, d)
            for r, q, s, n in spans(d):
                yield pltpu.make_async_copy(
                    x.at[2 * i + r, pl.ds(s, n)], xc.at[kind, d + REACH, r, pl.ds(q, n)], load_c.at[kind]
                )

    for kind in range(2):
        for copy in class_loads(kind):
            copy.start()

    def big_load(i):
        return pltpu.make_async_copy(x.at[pl.ds(2 * i, 2)], xs.at[pl.ds(2 * i, 2)], load_x.at[i])

    for i in range(8):
        big_load(i).start()

    for ref in (xr, tr):
        ref[1, pl.ds(layer * SB, SB), :] = jnp.zeros((SB, SB), jnp.bfloat16)

    barrier = pltpu.get_barrier_semaphore()
    for there in (above, below):
        pl.semaphore_signal(barrier, inc=1, device_id=there, device_id_type=MESH)
    for k in range(1, layers):
        there = (row, col, lax.rem(layer + k, layers))
        pl.semaphore_signal(barrier, inc=1, device_id=there, device_id_type=MESH)
    pl.semaphore_wait(barrier, 2 + layers - 1)

    def halo(ref, send, recv, kind, d):
        i, c = place(layer, kind, d)

        def copy(to, c_there, i_there, n):
            high, wide = (SB // 2, BS) if d == REACH else (SB, SB)
            shift = SB - high
            return pltpu.make_async_remote_copy(
                src_ref=ref.at[c, pl.ds((i + 4) * SB + shift, high), pl.ds(0, wide)],
                dst_ref=ref.at[c_there, pl.ds(i_there * SB + shift, high), pl.ds(0, wide)],
                send_sem=send.at[n, kind, d + REACH],
                recv_sem=recv.at[n, kind, d + REACH],
                device_id=to,
                device_id_type=MESH,
            )

        if d > -REACH:
            yield (c >= 2) & (i >= 4), lambda: copy(above, c - 2, i - 4, 0)
        if d < REACH:
            yield (c <= 1) & (i <= 3), lambda: copy(below, c + 2, i + 12, 1)

    def halo_do(ref, send, recv, kind, d, act):
        for cond, make in halo(ref, send, recv, kind, d):
            pl.when(cond)(functools.partial(lambda make: getattr(make(), act)(), make))

    def masked(block, k):
        return block * jnp.full(block.shape, k, jnp.float32).astype(jnp.bfloat16)

    for kind in range(2):
        pltpu.make_async_copy(x.at[pl.ds(0, 2)], xs.at[pl.ds(0, 2)], load_c.at[kind]).wait()
        for d in DIAGS:
            i, c = place(layer, kind, d)
            if abs(d) == REACH:
                xr[c, pl.ds((i + 4) * SB, SB), :] = jnp.zeros((SB, SB), jnp.bfloat16)
            for r, q0, s0, n in spans(d):
                for q, s in zip(range(q0, q0 + n), range(s0, s0 + n)):
                    xr[c, pl.ds((i + 4) * SB + r * BS, BS), pl.ds(q * BS, BS)] = masked(
                        xc[kind, d + REACH, r, q], keep(2 * i + r, s)
                    )
            halo_do(xr, send_x, recv_x, kind, d, "start")

    def fill(i, _):
        big_load(i).wait()
        none = jnp.zeros((BS, BS), jnp.bfloat16)
        for r in range(2):
            for s in range(W):
                xl[i, pl.ds(r * BS, BS), pl.ds((r + s) * BS, BS)] = masked(xs[2 * i + r, s], keep(2 * i + r, s))
        xl[i, pl.ds(0, BS), pl.ds(16 * BS, BS)] = none
        xl[i, pl.ds(0, BS), pl.ds(17 * BS, BS)] = none
        xl[i, pl.ds(BS, BS), pl.ds(0, BS)] = none
        xl[i, pl.ds(BS, BS), pl.ds(17 * BS, BS)] = none
        return 0

    lax.fori_loop(0, 8, fill, 0)

    def product(ref, i, c, d):
        n, first = 9 - abs(d), max(d, 0)
        return jnp.dot(
            xl[i, :, pl.ds(first * SB, n * SB)],
            ref[c, pl.ds((i + first) * SB, n * SB), :],
            preferred_element_type=jnp.float32,
        )

    rows_at = lax.broadcasted_iota(jnp.int32, (BS, BS), 0)
    cols_at = lax.broadcasted_iota(jnp.int32, (BS, BS), 1)

    def first_product(kind, _):
        for d in DIAGS:
            halo_do(xr, send_x, recv_x, kind, d, "wait_recv")
        three = jnp.where(rows_at == cols_at, jnp.float32(3.0), jnp.float32(0.0))
        for d in DIAGS:
            i, c = place(layer, kind, d)
            total = product(xr, i, c, d)
            if abs(d) == REACH:
                tr[c, pl.ds((i + 4) * SB, SB), :] = jnp.zeros((SB, SB), jnp.bfloat16)
            for r, q0, s0, n in spans(d):
                for q, s in zip(range(q0, q0 + n), range(s0, s0 + n)):
                    part = total[r * BS : (r + 1) * BS, q * BS : (q + 1) * BS]
                    part = three - part if s == W // 2 else part * -keep(2 * i + r, s)
                    tr[c, pl.ds((i + 4) * SB + r * BS, BS), pl.ds(q * BS, BS)] = part.astype(jnp.bfloat16)
            halo_do(tr, send_t, recv_t, kind, d, "start")
        return 0

    lax.fori_loop(0, 2, first_product, 0)

    def second_product(kind, _):
        for d in DIAGS:
            halo_do(tr, send_t, recv_t, kind, d, "wait_recv")
        for d in DIAGS:
            i, c = place(layer, kind, d)
            total = product(tr, i, c, d)
            owner = i >> 1
            for r, q0, s0, n in spans(d):
                for q, s in zip(range(q0, q0 + n), range(s0, s0 + n)):
                    part = total[r * BS : (r + 1) * BS, q * BS : (q + 1) * BS]
                    os[kind, d + REACH, r, q] = (part * (0.5 * keep(2 * i + r, s))).astype(jnp.bfloat16)

            @pl.when(owner == layer)
            def _():
                for r, q, s, n in spans(d):
                    pltpu.make_async_copy(
                        os.at[kind, d + REACH, r, pl.ds(q, n)], out.at[2 * (i & 1) + r, pl.ds(s, n)], own_o
                    ).start()

            @pl.when(owner != layer)
            def _():
                for r, q, s, n in spans(d):
                    pltpu.make_async_remote_copy(
                        src_ref=os.at[kind, d + REACH, r, pl.ds(q, n)],
                        dst_ref=out.at[2 * (i & 1) + r, pl.ds(s, n)],
                        send_sem=send_o,
                        recv_sem=recv_o,
                        device_id=(row, col, owner),
                        device_id_type=MESH,
                    ).start()
        return 0

    lax.fori_loop(0, 2, second_product, 0)

    pltpu.make_async_copy(xs.at[pl.ds(0, 1)], out.at[pl.ds(0, 1)], own_o).wait()
    pltpu.make_async_copy(xs.at[pl.ds(0, 3)], out.at[pl.ds(0, 3)], send_o).wait()
    pltpu.make_async_copy(xs.at[pl.ds(0, 3)], out.at[pl.ds(0, 3)], recv_o).wait()

    def sent(kind, _):
        for d in DIAGS:
            halo_do(xr, send_x, recv_x, kind, d, "wait_send")
            halo_do(tr, send_t, recv_t, kind, d, "wait_send")
        return 0

    lax.fori_loop(0, 2, sent, 0)


def per_device(blocks, flags):
    halos = pltpu.SemaphoreType.DMA((2, 2, 9))
    return pl.pallas_call(
        kernel,
        out_shape=jax.ShapeDtypeStruct((4, W, BS, BS), jnp.bfloat16),
        in_specs=[pl.BlockSpec(memory_space=pl.ANY), pl.BlockSpec(memory_space=pltpu.SMEM)],
        out_specs=pl.BlockSpec(memory_space=pl.ANY),
        scratch_shapes=[
            pltpu.VMEM((2, 9, 2, 2, BS, BS), jnp.bfloat16),
            pltpu.VMEM((16, W, BS, BS), jnp.bfloat16),
            pltpu.VMEM((8, SB, 9 * SB), jnp.bfloat16),
            pltpu.VMEM((4, 16 * SB, SB), jnp.bfloat16),
            pltpu.VMEM((4, 16 * SB, SB), jnp.bfloat16),
            pltpu.VMEM((2, 9, 2, 2, BS, BS), jnp.bfloat16),
            pltpu.SemaphoreType.DMA((2,)),
            pltpu.SemaphoreType.DMA((8,)),
            halos,
            halos,
            halos,
            halos,
            pltpu.SemaphoreType.DMA,
            pltpu.SemaphoreType.DMA,
            pltpu.SemaphoreType.DMA,
        ],
        compiler_params=pltpu.CompilerParams(
            collective_id=0, has_side_effects=True, vmem_limit_bytes=56 * 2**20
        ),
        cost_estimate=pl.CostEstimate(
            flops=2 * 2 * 122 * SB**3, bytes_accessed=10 * 2**20, transcendentals=0
        ),
    )(blocks, flags)


def solution(mesh):
    return jax.shard_map(
        per_device,
        mesh=mesh,
        in_specs=(P(("row", "col"), None, None, None), P(("row", "col"), None)),
        out_specs=P(("row", "col", "layer"), None, None, None),
        check_vma=False,
    )
```

time: 706 us -> 58.6 us (0.08)
  waiting for transfers between devices: 407 us -> 0 us
  matrix products: 115 us -> 0 us
  other arithmetic: 112 us -> 0 us
  Pallas kernels: 0 us -> 55.1 us
  local copies, waits for them, and re-layouts: 47.4 us -> 3.16 us
  between operations: 13.1 us -> 0.01 us
  starting transfers between devices: 10.2 us -> 0 us
    reduce_scatter x2 -> x0, waiting for transfers between devices: 231 us -> none  [the longest x1 149 us: per_device(): lax.psum_scatter(term * keep_wide, 'layer', scatter_dimension=0, tiled=True)]
    dot_general x8 -> x0, matrix products: 115 us -> none  [step(): jnp.einsum('nxy,nsyz->nsxz', piece, moved, preferred_element_type=jnp.flo...]
    ppermute x4 -> x0, waiting for transfers between devices: 93 us -> none  [the longest x2 93 us: padded_2(): lax.ppermute(lax.slice_in_dim(block, block.shape[dim] - width, None, axis...]
    all_gather x1 -> x0, waiting for transfers between devices: 83 us -> none  [per_device(): third = lax.all_gather(third_own, 'layer', axis=0, tiled=True)]
    concatenate x2 -> x0, other arithmetic: 75.2 us -> none  [padded_2(): block = jnp.concatenate([low, block, high], axis=dim)]
    pallas_call x0 -> x1, Pallas kernels: none -> 55.1 us  [per_device(): pl.pallas_call(kernel, out_shape=jax.ShapeDtypeStruct((4, W, BS, BS), jnp...]
    while x2 -> x0, local copies, waits for them, and re-layouts: 35.3 us -> none  [banded_part(): return lax.fori_loop(0, offsets, step, start)]
    mul x3 -> x0, other arithmetic: 18.7 us -> none  [the longest x1 11.4 us: per_device(): term * keep_wide]
  transfers between devices with their start and end apart: 7 -> 0, of which waited for: 5 -> 0; matrix products, arithmetic and copies ran while one was open for 0% -> 0% of each run, Pallas kernels for 0% -> 0%
where the time goes in v1:
time: 58.6 us; the launch traced here: 58.3 us
  Pallas kernels  55.1 us (94%)
  local copies, waits for them, and re-layouts  3.16 us (5%)
    pallas_call x1, Pallas kernels, per_device(): pl.pallas_call(kernel, out_shape=jax.ShapeDtypeStruct((4, W, BS, BS), jnp...  55.1 us
    unnamed x1, local copies, waits for them, and re-layouts  3.16 us

profile of v1, /device:TPU:0, one launch (start us, length us, event | category | flops | bytes accessed | tf_op | source)
XLA Modules:
  0.0 58.3 jit_solution(16886661469749124425)
XLA Ops:
  0.0 55.1 %shard_map.28 = bf16[4,16,128,128]{3,2,1,0:T(8,128)(2,1)} custom-call(bf16[16,16,128,128]{3,2,1,0:T(8,128)(2,1)} %x.1, s32[16,16]{1,0:T(8,128)} %flags.1), custom_call_target="tpu_custom_call" | custom-call | flops 8187281408 | bytes 10485760 | tf_op jit(solution)/shard_map/pallas_call | solution.py:211
  55.1 3.2 %copy.4 = bf16[4,16,128,128]{3,2,1,0:T(8,128)(2,1)} copy(bf16[4,16,128,128]{3,2,1,0:T(8,128)(2,1)} %shard_map.28) | data formatting | bytes 4194304

commit v2 on v1

v2 whole, which is shorter than its diff:
```python
import functools

import jax
import jax.numpy as jnp
from jax import lax
from jax.experimental import pallas as pl
from jax.experimental.pallas import tpu as pltpu
from jax.sharding import PartitionSpec as P

MESH = pl.DeviceIdType.MESH
REACH = 4
DIAGS = range(-REACH, REACH + 1)
BS = 128
SB = 256
W = 16
ROWS = 16


ORDERS = (
    ((3, 0), (2, 0), (1, 0), (3, 1), (2, 1), (0, 0), (1, 1), (0, 1)),
    ((0, 0), (1, 0), (3, 0), (0, 1), (1, 1), (2, 0), (3, 1), (2, 1)),
)


def place(layer, kind, d):
    m = (d - layer + 3) >> 2
    t = (m + kind) & 1
    return layer - d + 4 * m + 4 * t, 1 + m + t


def spans(d):
    out = []
    for r in range(2):
        low, high = 2 * d - r + 8, 2 * d - r + 10
        first, last = max(low, 0), min(high, W)
        if last > first:
            out.append((r, first - low, first, last - first))
    return out


def cells(d):
    return [(r, q0 + k, s0 + k) for r, q0, s0, n in spans(d) for k in range(n)]


def chain(layer, c):
    middle = layer - 4 + 4 * c
    return [(1 - c % 2, middle - i) for i in range(max(middle - 4, 0), min(middle + 4, 7) + 1)]


def way_of(layer, kind, d):
    i, c = place(layer, kind, d)
    if c >= 2 and i >= 4:
        return 0, c - 2, i - 8
    if c <= 1 and i <= 3:
        return 1, c + 2, i + 8
    return None


def kernel(
    x, flags, flags_any, out, hx, xs, xl, right, res, flags_by, load_x,
    send_f, recv_f, send_x, recv_x, send_t, recv_t, send_o, recv_o, own_o,
):
    row, col, layer = lax.axis_index("row"), lax.axis_index("col"), lax.axis_index("layer")
    cols, layers = lax.axis_size("col"), lax.axis_size("layer")
    groups = lax.axis_size("row") * cols
    group = row * cols + col

    def at_group(step):
        there = lax.rem(group + step + groups, groups)
        return there // cols, lax.rem(there, cols), layer

    sides = at_group(1), at_group(-1)

    def keep(i, s):
        return jnp.float32(1.0) if s == W // 2 else flags[i, s].astype(jnp.float32)

    def big_load(i):
        return pltpu.make_async_copy(x.at[pl.ds(2 * i, 2)], xs.at[pl.ds(2 * i, 2)], load_x.at[i])

    def remote(src, dst, send, recv, to):
        return pltpu.make_async_remote_copy(
            src_ref=src, dst_ref=dst, send_sem=send, recv_sem=recv, device_id=to, device_id_type=MESH
        )

    def flag_halo(way):
        return remote(flags_any, flags_by.at[way], send_f.at[way], recv_f.at[way], sides[way])

    def masked(block, k):
        return block * jnp.full(block.shape, k, jnp.float32).astype(jnp.bfloat16)

    for p in range(2):
        right[p, 1, pl.ds(layer * SB, SB), :] = jnp.zeros((SB, SB), jnp.bfloat16)
        right[p, 3, pl.ds(15 * SB + BS, BS), :] = jnp.zeros((BS, SB), jnp.bfloat16)
        right[p, 2, pl.ds((layer + 12) * SB, SB), :] = jnp.zeros((SB, SB), jnp.bfloat16)

    barrier = pltpu.get_barrier_semaphore()
    for there in sides:
        pl.semaphore_signal(barrier, inc=1, device_id=there, device_id_type=MESH)
    for k in range(1, layers):
        there = (row, col, lax.rem(layer + k, layers))
        pl.semaphore_signal(barrier, inc=1, device_id=there, device_id_type=MESH)
    pl.semaphore_wait(barrier, 2 + layers - 1)

    rows_at = lax.broadcasted_iota(jnp.int32, (BS, BS), 0)
    cols_at = lax.broadcasted_iota(jnp.int32, (BS, BS), 1)

    class Share:
        def __init__(self, l):
            self.l = l

        def x_copies(self, kind, d):
            if way_of(self.l, kind, d) is None:
                return
            i, _ = place(self.l, kind, d)
            way, _, i_there = way_of(self.l, kind, d)
            for r, q, s, n in spans(d):
                if way == 1 and 2 * i + r == 7:
                    continue
                if way == 1 and self.l == 3 and kind == 0:
                    n = 1
                yield remote(
                    x.at[2 * i + r, pl.ds(s, n)],
                    hx.at[kind, d + REACH, r, pl.ds(q, n)],
                    send_x.at[kind, d + REACH, r],
                    recv_x.at[kind, d + REACH, r],
                    sides[way],
                ), [(r, q + k, s + k) for k in range(n)]

        def x_send(self, c):
            for kind, d in chain(self.l, c):
                for copy, _ in self.x_copies(kind, d):
                    copy.start()

        def x_take(self, c):
            for kind, d in chain(self.l, (c + 2) % 4):
                for copy, brought in self.x_copies(kind, d):
                    i, _ = place(self.l, kind, d)
                    way, c_there, i_there = way_of(self.l, kind, d)
                    copy.wait_recv()
                    for r, q, s in brought:
                        k = jnp.float32(1.0) if s == W // 2 else flags_by[way, 2 * i + r, s].astype(jnp.float32)
                        at = (i_there + 4) * SB + r * BS
                        right[0, c_there, at : at + BS, q * BS : (q + 1) * BS] = masked(hx[kind, d + REACH, r, q], k)

        def t_copy(self, kind, d):
            i, c = place(self.l, kind, d)
            way, c_there, i_there = way_of(self.l, kind, d)
            first, high, wide = 0, SB, SB
            if d == REACH:
                first, high, wide = BS, BS, BS
            if way == 1 and i == 3:
                high = BS
            if way == 1 and self.l == 3 and kind == 0:
                wide = BS
            return remote(
                res.at[0, kind, d + REACH, pl.ds(first, high), pl.ds(0, wide)],
                right.at[1, c_there, pl.ds((i_there + 4) * SB + first, high), pl.ds(0, wide)],
                send_t.at[kind, d + REACH],
                recv_t.at[kind, d + REACH],
                sides[way],
            )

        def own_right(self):
            for kind in range(2):
                for d in DIAGS:
                    i, c = place(self.l, kind, d)
                    right[0, c, (i + 4) * SB : (i + 5) * SB, :] = xl[i, :, (d + REACH) * SB : (d + REACH + 1) * SB]

        def task(self, p, kind, d):
            i, c = place(self.l, kind, d)
            n, first = 9 - abs(d), max(d, 0)
            total = jnp.dot(
                xl[i, :, first * SB : (first + n) * SB],
                right[p, c, (i + first) * SB : (i + first + n) * SB, :],
                preferred_element_type=jnp.float32,
            )
            scale = jnp.where(p == 0, jnp.float32(-1.0), jnp.float32(0.5))
            three = jnp.where(rows_at == cols_at, jnp.where(p == 0, jnp.float32(3.0), jnp.float32(0.0)), jnp.float32(0.0))
            if abs(d) == REACH:
                res[p, kind, d + REACH] = jnp.zeros((SB, SB), jnp.bfloat16)
            for r, q, s in cells(d):
                part = total[r * BS : (r + 1) * BS, q * BS : (q + 1) * BS]
                part = part * scale + three if s == W // 2 else part * (scale * keep(2 * i + r, s))
                res[p, kind, d + REACH, r * BS : (r + 1) * BS, q * BS : (q + 1) * BS] = part.astype(jnp.bfloat16)

        def third_out(self, c):
            for kind, d in chain(self.l, c):
                if way_of(self.l, kind, d):
                    self.t_copy(kind, d).start()
            for kind, d in chain(self.l, c):
                i, _ = place(self.l, kind, d)
                right[1, c, (i + 4) * SB : (i + 5) * SB, :] = res[0, kind, d + REACH]

        def result_out(self, c):
            for kind, d in chain(self.l, c):
                i, _ = place(self.l, kind, d)
                for r, q, s in cells(d):
                    src = res.at[1, kind, d + REACH, pl.ds(r * BS, BS), pl.ds(q * BS, BS)]
                    dst = out.at[2 * (i & 1) + r, s]
                    if i >> 1 == self.l:
                        pltpu.make_async_copy(src, dst, own_o).start()
                    else:
                        remote(src, dst, send_o, recv_o, (row, col, i >> 1)).start()

        def t_take(self, c):
            for at in chain(self.l, (c + 2) % 4):
                if way_of(self.l, *at):
                    self.t_copy(*at).wait_recv()

        def start(self):
            def step(at, _):
                turn = jnp.where(core == 0, pick(at, (1, 3, 2, 0)), pick(at, (3, 0, 1, 2)))
                for c in range(4):
                    pl.when(turn == c)(functools.partial(self.x_send, c))
                return 0

            lax.fori_loop(0, 4, step, 0)

        def block(self, c, p):
            pl.when(p == 0)(functools.partial(self.x_take, c))
            pl.when(p == 1)(functools.partial(self.t_take, c))
            for kind, d in chain(self.l, c):
                self.task(p, kind, d)
            pl.when(p == 0)(functools.partial(self.third_out, c))
            pl.when(p == 1)(functools.partial(self.result_out, c))

        def run(self):
            self.own_right()

            def step(at, _):
                turn = [pick(at, [(c + 4 * p) for c, p in order]) for order in ORDERS]
                turn = jnp.where(core == 0, *turn)
                for c in range(4):
                    pl.when((turn & 3) == c)(functools.partial(self.block, c, turn >> 2))
                return 0

            lax.fori_loop(0, 8, step, 0)
            for c in range(4):
                for kind, d in chain(self.l, c):
                    for copy, _ in self.x_copies(kind, d):
                        copy.wait_send()
                    if way_of(self.l, kind, d):
                        self.t_copy(kind, d).wait_send()

    core = lax.rem(col, 2)

    def pick(at, values):
        out = jnp.int32(values[-1])
        for k, value in enumerate(values[:-1]):
            out = jnp.where(at == k, jnp.int32(value), out)
        return out

    def each_share(act):
        for l in range(4):
            pl.when(layer == l)(functools.partial(act, Share(l)))

    flag_halo(0).start()
    flag_halo(1).start()

    each_share(Share.start)
    for i in range(8):
        big_load(i).start()

    def fill(i, _):
        big_load(i).wait()
        none = jnp.zeros((BS, BS), jnp.bfloat16)
        for r in range(2):
            for s in range(W):
                xl[i, pl.ds(r * BS, BS), pl.ds((r + s) * BS, BS)] = masked(xs[2 * i + r, s], keep(2 * i + r, s))
        xl[i, pl.ds(0, BS), pl.ds(16 * BS, BS)] = none
        xl[i, pl.ds(0, BS), pl.ds(17 * BS, BS)] = none
        xl[i, pl.ds(BS, BS), pl.ds(0, BS)] = none
        xl[i, pl.ds(BS, BS), pl.ds(17 * BS, BS)] = none
        return 0

    lax.fori_loop(0, 8, fill, 0)
    flag_halo(0).wait()
    flag_halo(1).wait()

    each_share(Share.run)

    pltpu.make_async_copy(xs.at[pl.ds(0, 1)], out.at[pl.ds(0, 1)], own_o).wait()
    pltpu.make_async_copy(xs.at[pl.ds(0, 3)], out.at[pl.ds(0, 3)], send_o).wait()
    pltpu.make_async_copy(xs.at[pl.ds(0, 3)], out.at[pl.ds(0, 3)], recv_o).wait()


def per_device(blocks, flags):
    return pl.pallas_call(
        kernel,
        out_shape=jax.ShapeDtypeStruct((4, W, BS, BS), jnp.bfloat16),
        in_specs=[
            pl.BlockSpec(memory_space=pl.ANY),
            pl.BlockSpec(memory_space=pltpu.SMEM),
            pl.BlockSpec(memory_space=pl.ANY),
        ],
        out_specs=pl.BlockSpec(memory_space=pl.ANY),
        scratch_shapes=[
            pltpu.VMEM((2, 9, 2, 2, BS, BS), jnp.bfloat16),
            pltpu.VMEM((ROWS, W, BS, BS), jnp.bfloat16),
            pltpu.VMEM((8, SB, 9 * SB), jnp.bfloat16),
            pltpu.VMEM((2, 4, 16 * SB, SB), jnp.bfloat16),
            pltpu.VMEM((2, 2, 9, SB, SB), jnp.bfloat16),
            pltpu.SMEM((2, ROWS, W), jnp.int32),
            pltpu.SemaphoreType.DMA((8,)),
            pltpu.SemaphoreType.DMA((2,)),
            pltpu.SemaphoreType.DMA((2,)),
            pltpu.SemaphoreType.DMA((2, 9, 2)),
            pltpu.SemaphoreType.DMA((2, 9, 2)),
            pltpu.SemaphoreType.DMA((2, 9)),
            pltpu.SemaphoreType.DMA((2, 9)),
            pltpu.SemaphoreType.DMA,
            pltpu.SemaphoreType.DMA,
            pltpu.SemaphoreType.DMA,
        ],
        compiler_params=pltpu.CompilerParams(
            collective_id=0, has_side_effects=True, vmem_limit_bytes=56 * 2**20
        ),
        cost_estimate=pl.CostEstimate(
            flops=2 * 2 * 122 * SB**3, bytes_accessed=10 * 2**20, transcendentals=0
        ),
    )(blocks, flags, flags)


def solution(mesh):
    return jax.shard_map(
        per_device,
        mesh=mesh,
        in_specs=(P(("row", "col"), None, None, None), P(("row", "col"), None)),
        out_specs=P(("row", "col", "layer"), None, None, None),
        check_vma=False,
    )
```

time: 58.6 us -> 46.7 us (0.80)
  Pallas kernels: 55.1 us -> 43.4 us
    pallas_call x1, Pallas kernels: 55.1 us -> 43.4 us  [per_device(): pl.pallas_call(kernel, out_shape=jax.ShapeDtypeStruct((4, W, BS, BS), jnp...]
where the time goes in v2:
time: 46.7 us; the launch traced here: 46.6 us
  Pallas kernels  43.4 us (93%)
  local copies, waits for them, and re-layouts  3.16 us (7%)
    pallas_call x1, Pallas kernels, per_device(): pl.pallas_call(kernel, out_shape=jax.ShapeDtypeStruct((4, W, BS, BS), jnp...  43.4 us
    unnamed x1, local copies, waits for them, and re-layouts  3.16 us

profile of v2, /device:TPU:0, one launch (start us, length us, event | category | flops | bytes accessed | tf_op | source)
XLA Modules:
  0.0 46.6 jit_solution(14175730894384517001)
XLA Ops:
  0.0 43.4 %shard_map.28 = bf16[4,16,128,128]{3,2,1,0:T(8,128)(2,1)} custom-call(bf16[16,16,128,128]{3,2,1,0:T(8,128)(2,1)} %x.1, s32[16,16]{1,0:T(8,128)} %flags_any.1, s32[16,16]{1,0:T(8,128)} %flags_any.1), custom_call_target="tpu_custom_call" | custom-call | flops 8187281408 | bytes 10485760 | tf_op jit(solution)/shard_map/pallas_call | solution.py:288
  43.4 3.2 %copy.4 = bf16[4,16,128,128]{3,2,1,0:T(8,128)(2,1)} copy(bf16[4,16,128,128]{3,2,1,0:T(8,128)(2,1)} %shard_map.28) | data formatting | bytes 4194304

commit v3 on v2

--- a/solution.py
+++ b/solution.py
@@ -17,8 +17,8 @@
 
 
 ORDERS = (
-    ((3, 0), (2, 0), (1, 0), (3, 1), (2, 1), (0, 0), (1, 1), (0, 1)),
-    ((0, 0), (1, 0), (3, 0), (0, 1), (1, 1), (2, 0), (3, 1), (2, 1)),
+    ((3, 0), (2, 0), (2, 1), (1, 0), (3, 1), (0, 0), (1, 1), (0, 1)),
+    ((0, 0), (1, 0), (1, 1), (3, 0), (0, 1), (2, 0), (3, 1), (2, 1)),
 )
 
 
@@ -57,8 +57,8 @@
 
 
 def kernel(
-    x, flags, flags_any, out, hx, xs, xl, right, res, flags_by, load_x,
-    send_f, recv_f, send_x, recv_x, send_t, recv_t, send_o, recv_o, own_o,
+    x, flags_any, out, hx, xs, xl, right, res, flags, flags_by, load_x,
+    send_f, recv_f, send_x, recv_x, send_t, recv_t, send_o, recv_o, own_o, own_f, answer, told,
 ):
     row, col, layer = lax.axis_index("row"), lax.axis_index("col"), lax.axis_index("layer")
     cols, layers = lax.axis_size("col"), lax.axis_size("layer")
@@ -88,18 +88,46 @@
     def masked(block, k):
         return block * jnp.full(block.shape, k, jnp.float32).astype(jnp.bfloat16)
 
+    own_flags = pltpu.make_async_copy(flags_any, flags, own_f)
+    own_flags.start()
+    for i in range(8):
+        big_load(i).start()
+
     for p in range(2):
         right[p, 1, pl.ds(layer * SB, SB), :] = jnp.zeros((SB, SB), jnp.bfloat16)
         right[p, 3, pl.ds(15 * SB + BS, BS), :] = jnp.zeros((BS, SB), jnp.bfloat16)
         right[p, 2, pl.ds((layer + 12) * SB, SB), :] = jnp.zeros((SB, SB), jnp.bfloat16)
 
     barrier = pltpu.get_barrier_semaphore()
-    for there in sides:
-        pl.semaphore_signal(barrier, inc=1, device_id=there, device_id_type=MESH)
-    for k in range(1, layers):
-        there = (row, col, lax.rem(layer + k, layers))
-        pl.semaphore_signal(barrier, inc=1, device_id=there, device_id_type=MESH)
-    pl.semaphore_wait(barrier, 2 + layers - 1)
+    core = lax.rem(col, 2)
+
+    @pl.when(core == 0)
+    def _():
+        for there in sides:
+            pl.semaphore_signal(barrier, inc=1, device_id=there, device_id_type=MESH)
+
+    @pl.when(core == 1)
+    def _():
+        pl.semaphore_wait(barrier, 2)
+        for there in sides:
+            pl.semaphore_signal(answer, inc=1, device_id=there, device_id_type=MESH)
+
+    @pl.when(core == 0)
+    def _():
+        pl.semaphore_wait(answer, 2)
+        for k in range(1, layers):
+            there = (row, col, lax.rem(layer + k, layers))
+            pl.semaphore_signal(barrier, inc=1, device_id=there, device_id_type=MESH)
+
+    def at_layers():
+        @pl.when(core == 0)
+        def _():
+            pl.semaphore_wait(barrier, layers - 1)
+            pl.semaphore_signal(told, inc=1, device_id=sides[0], device_id_type=MESH)
+
+        @pl.when(core == 1)
+        def _():
+            pl.semaphore_wait(told, 1)
 
     rows_at = lax.broadcasted_iota(jnp.int32, (BS, BS), 0)
     cols_at = lax.broadcasted_iota(jnp.int32, (BS, BS), 1)
@@ -153,7 +181,7 @@
             if way == 1 and self.l == 3 and kind == 0:
                 wide = BS
             return remote(
-                res.at[0, kind, d + REACH, pl.ds(first, high), pl.ds(0, wide)],
+                right.at[1, c, pl.ds((i + 4) * SB + first, high), pl.ds(0, wide)],
                 right.at[1, c_there, pl.ds((i_there + 4) * SB + first, high), pl.ds(0, wide)],
                 send_t.at[kind, d + REACH],
                 recv_t.at[kind, d + REACH],
@@ -176,27 +204,30 @@
             )
             scale = jnp.where(p == 0, jnp.float32(-1.0), jnp.float32(0.5))
             three = jnp.where(rows_at == cols_at, jnp.where(p == 0, jnp.float32(3.0), jnp.float32(0.0)), jnp.float32(0.0))
-            if abs(d) == REACH:
-                res[p, kind, d + REACH] = jnp.zeros((SB, SB), jnp.bfloat16)
             for r, q, s in cells(d):
                 part = total[r * BS : (r + 1) * BS, q * BS : (q + 1) * BS]
                 part = part * scale + three if s == W // 2 else part * (scale * keep(2 * i + r, s))
-                res[p, kind, d + REACH, r * BS : (r + 1) * BS, q * BS : (q + 1) * BS] = part.astype(jnp.bfloat16)
+                res[p, kind, d + REACH, r, q] = part.astype(jnp.bfloat16)
 
         def third_out(self, c):
-            for kind, d in chain(self.l, c):
+            todo = chain(self.l, c)
+            todo.sort(key=lambda at: way_of(self.l, *at) is None)
+            for kind, d in todo:
+                i, _ = place(self.l, kind, d)
+                if abs(d) == REACH:
+                    right[1, c, (i + 4) * SB : (i + 5) * SB, :] = jnp.zeros((SB, SB), jnp.bfloat16)
+                for r, q, _ in cells(d):
+                    at = (i + 4) * SB + r * BS
+                    right[1, c, at : at + BS, q * BS : (q + 1) * BS] = res[0, kind, d + REACH, r, q]
                 if way_of(self.l, kind, d):
                     self.t_copy(kind, d).start()
-            for kind, d in chain(self.l, c):
-                i, _ = place(self.l, kind, d)
-                right[1, c, (i + 4) * SB : (i + 5) * SB, :] = res[0, kind, d + REACH]
 
         def result_out(self, c):
             for kind, d in chain(self.l, c):
                 i, _ = place(self.l, kind, d)
-                for r, q, s in cells(d):
-                    src = res.at[1, kind, d + REACH, pl.ds(r * BS, BS), pl.ds(q * BS, BS)]
-                    dst = out.at[2 * (i & 1) + r, s]
+                for r, q, s, n in spans(d):
+                    src = res.at[1, kind, d + REACH, r, pl.ds(q, n)]
+                    dst = out.at[2 * (i & 1) + r, pl.ds(s, n)]
                     if i >> 1 == self.l:
                         pltpu.make_async_copy(src, dst, own_o).start()
                     else:
@@ -230,6 +261,7 @@
             def step(at, _):
                 turn = [pick(at, [(c + 4 * p) for c, p in order]) for order in ORDERS]
                 turn = jnp.where(core == 0, *turn)
+                pl.when(at == 2)(at_layers)
                 for c in range(4):
                     pl.when((turn & 3) == c)(functools.partial(self.block, c, turn >> 2))
                 return 0
@@ -242,8 +274,6 @@
                     if way_of(self.l, kind, d):
                         self.t_copy(kind, d).wait_send()
 
-    core = lax.rem(col, 2)
-
     def pick(at, values):
         out = jnp.int32(values[-1])
         for k, value in enumerate(values[:-1]):
@@ -258,8 +288,6 @@
     flag_halo(1).start()
 
     each_share(Share.start)
-    for i in range(8):
-        big_load(i).start()
 
     def fill(i, _):
         big_load(i).wait()
@@ -273,6 +301,7 @@
         xl[i, pl.ds(BS, BS), pl.ds(17 * BS, BS)] = none
         return 0
 
+    own_flags.wait()
     lax.fori_loop(0, 8, fill, 0)
     flag_halo(0).wait()
     flag_halo(1).wait()
@@ -290,7 +319,6 @@
         out_shape=jax.ShapeDtypeStruct((4, W, BS, BS), jnp.bfloat16),
         in_specs=[
             pl.BlockSpec(memory_space=pl.ANY),
-            pl.BlockSpec(memory_space=pltpu.SMEM),
             pl.BlockSpec(memory_space=pl.ANY),
         ],
         out_specs=pl.BlockSpec(memory_space=pl.ANY),
@@ -299,7 +327,8 @@
             pltpu.VMEM((ROWS, W, BS, BS), jnp.bfloat16),
             pltpu.VMEM((8, SB, 9 * SB), jnp.bfloat16),
             pltpu.VMEM((2, 4, 16 * SB, SB), jnp.bfloat16),
-            pltpu.VMEM((2, 2, 9, SB, SB), jnp.bfloat16),
+            pltpu.VMEM((2, 2, 9, 2, 2, BS, BS), jnp.bfloat16),
+            pltpu.SMEM((ROWS, W), jnp.int32),
             pltpu.SMEM((2, ROWS, W), jnp.int32),
             pltpu.SemaphoreType.DMA((8,)),
             pltpu.SemaphoreType.DMA((2,)),
@@ -311,6 +340,9 @@
             pltpu.SemaphoreType.DMA,
             pltpu.SemaphoreType.DMA,
             pltpu.SemaphoreType.DMA,
+            pltpu.SemaphoreType.DMA,
+            pltpu.SemaphoreType.REGULAR,
+            pltpu.SemaphoreType.REGULAR,
         ],
         compiler_params=pltpu.CompilerParams(
             collective_id=0, has_side_effects=True, vmem_limit_bytes=56 * 2**20
@@ -318,7 +350,7 @@
         cost_estimate=pl.CostEstimate(
             flops=2 * 2 * 122 * SB**3, bytes_accessed=10 * 2**20, transcendentals=0
         ),
-    )(blocks, flags, flags)
+    )(blocks, flags)
 
 
 def solution(mesh):

time: 46.7 us -> 44.9 us (0.961)
  Pallas kernels: 43.4 us -> 41.6 us
    pallas_call x1, Pallas kernels: 43.4 us -> 41.6 us  [per_device(): pl.pallas_call(kernel, out_shape=jax.ShapeDtypeStruct((4, W, BS, BS), jnp...]
where the time goes in v3:
time: 44.9 us; the launch traced here: 44.8 us
  Pallas kernels  41.6 us (93%)
  local copies, waits for them, and re-layouts  3.16 us (7%)
    pallas_call x1, Pallas kernels, per_device(): pl.pallas_call(kernel, out_shape=jax.ShapeDtypeStruct((4, W, BS, BS), jnp...  41.6 us
    unnamed x1, local copies, waits for them, and re-layouts  3.16 us

profile of v3, /device:TPU:0, one launch (start us, length us, event | category | flops | bytes accessed | tf_op | source)
XLA Modules:
  0.0 44.8 jit_solution(12408940861480204366)
XLA Ops:
  0.0 41.6 %shard_map.28 = bf16[4,16,128,128]{3,2,1,0:T(8,128)(2,1)} custom-call(bf16[16,16,128,128]{3,2,1,0:T(8,128)(2,1)} %x.1, s32[16,16]{1,0:T(8,128)} %flags_any.1), custom_call_target="tpu_custom_call" | custom-call | flops 8187281408 | bytes 10485760 | tf_op jit(solution)/shard_map/pallas_call | solution.py:317
  41.6 3.2 %copy.4 = bf16[4,16,128,128]{3,2,1,0:T(8,128)(2,1)} copy(bf16[4,16,128,128]{3,2,1,0:T(8,128)(2,1)} %shard_map.28) | data formatting | bytes 4194304

commit v4 on v3

--- a/solution.py
+++ b/solution.py
@@ -17,8 +17,8 @@
 
 
 ORDERS = (
-    ((3, 0), (2, 0), (2, 1), (1, 0), (3, 1), (0, 0), (1, 1), (0, 1)),
-    ((0, 0), (1, 0), (1, 1), (3, 0), (0, 1), (2, 0), (3, 1), (2, 1)),
+    ((3, 0), (2, 0), (2, 1), (3, 1), (1, 0), (0, 0), (1, 1), (0, 1)),
+    ((0, 0), (1, 0), (1, 1), (0, 1), (3, 0), (2, 0), (3, 1), (2, 1)),
 )
 
 
@@ -313,7 +313,7 @@
     pltpu.make_async_copy(xs.at[pl.ds(0, 3)], out.at[pl.ds(0, 3)], recv_o).wait()
 
 
-def per_device(blocks, flags):
+def iterate(blocks, flags):
     return pl.pallas_call(
         kernel,
         out_shape=jax.ShapeDtypeStruct((4, W, BS, BS), jnp.bfloat16),
@@ -353,6 +353,34 @@
     )(blocks, flags)
 
 
+def settle(src, dst, held, sem_in, sem_out):
+    pieces = [(k // 2, pl.ds(k % 2 * 8, 8)) for k in range(8)]
+    reads = [pltpu.make_async_copy(src.at[at], held.at[at], sem_in.at[k]) for k, at in enumerate(pieces)]
+    writes = [pltpu.make_async_copy(held.at[at], dst.at[at], sem_out.at[k]) for k, at in enumerate(pieces)]
+    for read in reads:
+        read.start()
+    for read, write in zip(reads, writes):
+        read.wait()
+        write.start()
+    for write in writes:
+        write.wait()
+
+
+def per_device(blocks, flags):
+    result = iterate(blocks, flags)
+    return pl.pallas_call(
+        settle,
+        out_shape=jax.ShapeDtypeStruct(result.shape, result.dtype),
+        in_specs=[pl.BlockSpec(memory_space=pl.ANY)],
+        out_specs=pl.BlockSpec(memory_space=pl.ANY),
+        scratch_shapes=[
+            pltpu.VMEM(result.shape, result.dtype),
+            pltpu.SemaphoreType.DMA((8,)),
+            pltpu.SemaphoreType.DMA((8,)),
+        ],
+    )(result)
+
+
 def solution(mesh):
     return jax.shard_map(
         per_device,

time: 44.9 us -> 44.4 us (0.989)
  local copies, waits for them, and re-layouts: 3.16 us -> 0 us
  Pallas kernels: 41.6 us -> 44.1 us
    unnamed x1 -> x0, local copies, waits for them, and re-layouts: 3.16 us -> none
    pallas_call x1 -> x2, Pallas kernels: 41.6 us -> 44.1 us  [the longest x1 41.7 us: iterate(): pl.pallas_call(kernel, out_shape=jax.ShapeDtypeStruct((4, W, BS, BS), jnp...]
where the time goes in v4:
time: 44.4 us; the launch traced here: 44.3 us
  Pallas kernels  44.1 us (99%)
    pallas_call x1, Pallas kernels, iterate(): pl.pallas_call(kernel, out_shape=jax.ShapeDtypeStruct((4, W, BS, BS), jnp...  41.7 us
    pallas_call x1, Pallas kernels, per_device(): pl.pallas_call(settle, out_shape=jax.ShapeDtypeStruct(result.shape, resul...  2.39 us

profile of v4, /device:TPU:0, one launch (start us, length us, event | category | flops | bytes accessed | tf_op | source)
XLA Modules:
  0.0 44.3 jit_solution(16452639279647309216)
XLA Ops:
  0.0 41.7 %shard_map.28.src = bf16[4,16,128,128]{3,2,1,0:T(8,128)(2,1)} custom-call(bf16[16,16,128,128]{3,2,1,0:T(8,128)(2,1)} %x.1, s32[16,16]{1,0:T(8,128)} %flags_any.1), custom_call_target="tpu_custom_call" | custom-call | flops 8187281408 | bytes 10485760 | tf_op jit(solution)/shard_map/pallas_call | solution.py:317
  41.7 2.4 %shard_map.29 = bf16[4,16,128,128]{3,2,1,0:T(8,128)(2,1)} custom-call(bf16[4,16,128,128]{3,2,1,0:T(8,128)(2,1)} %shard_map.28.src), custom_call_target="tpu_custom_call" | custom-call | tf_op jit(solution)/shard_map/pallas_call | solution.py:371

commit v5 on v4

--- a/solution.py
+++ b/solution.py
@@ -240,7 +240,7 @@
 
         def start(self):
             def step(at, _):
-                turn = jnp.where(core == 0, pick(at, (1, 3, 2, 0)), pick(at, (3, 0, 1, 2)))
+                turn = jnp.where(core == 0, pick(at, (3, 2, 1, 0)), pick(at, (0, 1, 3, 2)))
                 for c in range(4):
                     pl.when(turn == c)(functools.partial(self.x_send, c))
                 return 0
@@ -250,7 +250,7 @@
         def block(self, c, p):
             pl.when(p == 0)(functools.partial(self.x_take, c))
             pl.when(p == 1)(functools.partial(self.t_take, c))
-            for kind, d in chain(self.l, c):
+            for kind, d in sorted(chain(self.l, c), key=lambda at: place(self.l, *at)[0] >> 1 == self.l):
                 self.task(p, kind, d)
             pl.when(p == 0)(functools.partial(self.third_out, c))
             pl.when(p == 1)(functools.partial(self.result_out, c))

time: 44.4 us -> 44.4 us (level)
  no operation moved by 1% of the time
where the time goes in v5:
time: 44.4 us; the launch traced here: 44.3 us
  Pallas kernels  44.1 us (99%)
    pallas_call x1, Pallas kernels, iterate(): pl.pallas_call(kernel, out_shape=jax.ShapeDtypeStruct((4, W, BS, BS), jnp...  41.7 us
    pallas_call x1, Pallas kernels, per_device(): pl.pallas_call(settle, out_shape=jax.ShapeDtypeStruct(result.shape, resul...  2.39 us

profile of v5, /device:TPU:0, one launch (start us, length us, event | category | flops | bytes accessed | tf_op | source)
XLA Modules:
  0.0 44.3 jit_solution(4518625378540558686)
XLA Ops:
  0.0 41.7 %shard_map.28.src = bf16[4,16,128,128]{3,2,1,0:T(8,128)(2,1)} custom-call(bf16[16,16,128,128]{3,2,1,0:T(8,128)(2,1)} %x.1, s32[16,16]{1,0:T(8,128)} %flags_any.1), custom_call_target="tpu_custom_call" | custom-call | flops 8187281408 | bytes 10485760 | tf_op jit(solution)/shard_map/pallas_call | solution.py:317
  41.7 2.4 %shard_map.29 = bf16[4,16,128,128]{3,2,1,0:T(8,128)(2,1)} custom-call(bf16[4,16,128,128]{3,2,1,0:T(8,128)(2,1)} %shard_map.28.src), custom_call_target="tpu_custom_call" | custom-call | tf_op jit(solution)/shard_map/pallas_call | solution.py:371
